TPU v7x, 1024 devices: a whole 4x8x16 slice. The times are simulated.
1024 devices in a mesh: dp: 16 (over z_hi, x), pipe: 16 (over y, core), mp: 4 (over z_lo).
Axes of the slice: x: 4, y: 8, z: 16 (z_hi: 4, z_lo: 4; z = z_hi * 4 + z_lo), core: 2. Of those that a mesh axis runs over, the one named last changes fastest.
Arguments:
- stash: bfloat16 [16, 16, 10, 64, 8192], P('pipe', 'dp', None, None, 'mp')
- own_input: bfloat16 [16, 16, 128, 8192], P('pipe', 'dp', None, 'mp')
- gain: bfloat16 [16, 8192], P('pipe', 'mp'), may hold values from 0.099609375 to 1.8984375
- key_weight: bfloat16 [16, 8192, 512], P('pipe', 'mp'), may hold values from -0.0625 to 0.0625
- own_cotangent: bfloat16 [16, 16, 128, 512], P('pipe', 'dp'), may hold values from -0.3125 to 0.3125
- replay_cotangent: bfloat16 [16, 16, 2, 64, 512], P('pipe', 'dp'), may hold values from -0.3125 to 0.3125
- failed: int32 [16], replicated, may hold values from 0 to 15
- counts: int32 [16, 16], replicated, may hold values from 0 to 2, as said below
- table: int32 [16, 16, 2], replicated, may hold values from 0 to 9, as said below
Outputs:
- replayed_keys: bfloat16 [16, 16, 2, 64, 512], P('pipe', 'dp', None, None, 'mp')
- weight_grad: float32 [16, 8192, 512], P('pipe', ('mp', 'dp'))
Inputs may be any that keep to these rules, and one draw needn't show every extreme that they name: Per section the counts sum to 10; the failed replica's count is 0; some replica of every section has exactly 2. `table`: per section, the first counts[s, r] entries of the replicas' rows name each of the 10 microbatches exactly once; later entries are arbitrary and unused.
All inputs are finite; a program needn't handle non-finite values.
Results may differ from a plain program's by a relative error of at most 0.02.
Values may be sent and summed in bfloat16 or wider, within the bound.
A program may use at most 32 MiB of HBM per device.

v0:
```python
import jax
import jax.numpy as jnp
from jax import lax
from jax.sharding import PartitionSpec as P

D = 8192


epsilon = 1e-05


def from_root(value, axis, source):
    kept = jnp.where(lax.axis_index(axis) == source, value, 0).astype(value.dtype)
    return lax.psum(kept, axis)


def from_behind(value, axis, steps):
    count = lax.axis_size(axis)
    pairs = [(source, (source + steps) % count) for source in range(count)]
    return lax.ppermute(value, axis, pairs)


def pick_slots(root_rows, slots, live):
    return jnp.where(live[:, None, None], root_rows[slots], jnp.zeros((), root_rows.dtype))


def per_device(
    stash, own_input, gain, key_weight, own_cotangent, replay_cotangent, failed, counts, table
):
    section_total = lax.axis_size("pipe")
    section_index = lax.axis_index("pipe")
    replica = lax.axis_index("dp")
    width_index = lax.axis_index("mp")
    slot_total = table.shape[2]
    slot_ids = jnp.arange(slot_total, dtype=jnp.int32)
    upcoming = (section_index + 1) % section_total
    root_rows = from_root(stash[0, 0], "dp", failed[upcoming])
    next_live = slot_ids < counts[upcoming, replica]
    picked = pick_slots(root_rows, table[upcoming, replica], next_live)
    arrived = from_behind(picked, "pipe", 1)
    token_total = arrived.shape[1]
    quarter = arrived.shape[2]
    scaling = gain[0].astype(jnp.float32)
    arrived_float = arrived.reshape(slot_total * token_total, quarter).astype(jnp.float32)
    mixed = (arrived_float * scaling).astype(jnp.bfloat16)
    squares_replay = jnp.sum(arrived_float * arrived_float, axis=1)
    own_float = own_input[0, 0].astype(jnp.float32)
    own_mixed = (own_float * scaling).astype(jnp.bfloat16)
    squares_own = jnp.sum(own_float * own_float, axis=1)
    weight = key_weight[0]
    partial_keys = jnp.dot(mixed, weight, preferred_element_type=jnp.float32)
    key_width = weight.shape[1]
    share = key_width // lax.axis_size("mp")
    summed_keys, total_replay, total_own = (
        lax.psum(partial_keys.astype(jnp.bfloat16), "mp").astype(jnp.float32),
        lax.psum(squares_replay.astype(jnp.bfloat16), "mp").astype(jnp.float32),
        lax.psum(squares_own.astype(jnp.bfloat16), "mp").astype(jnp.float32),
    )
    my_keys = lax.dynamic_slice_in_dim(summed_keys, width_index * share, share, 1)
    factor_replay = lax.rsqrt(total_replay / D + epsilon)
    factor_own = lax.rsqrt(total_own / D + epsilon)
    keys_here = (
        (my_keys * factor_replay[:, None])
        .astype(jnp.bfloat16)
        .reshape(slot_total, token_total, share)
    )
    passed = from_behind(keys_here, "pipe", 1)
    keeper = (replica != failed[section_index]).astype(jnp.float32)
    replay_float = (
        replay_cotangent[0, 0].reshape(slot_total * token_total, key_width).astype(jnp.float32)
    )
    replay_back = (replay_float * factor_replay[:, None]).astype(jnp.bfloat16)
    own_back = (own_cotangent[0, 0].astype(jnp.float32) * (factor_own * keeper)[:, None]).astype(
        jnp.bfloat16
    )
    contract = (((0,), (0,)), ((), ()))
    replay_part = lax.dot_general(mixed, replay_back, contract, preferred_element_type=jnp.float32)
    own_part = lax.dot_general(own_mixed, own_back, contract, preferred_element_type=jnp.float32)
    gradient = lax.psum_scatter(
        (replay_part + own_part).astype(jnp.bfloat16), "dp", scatter_dimension=0, tiled=True
    ).astype(jnp.float32)
    return (passed[None, None], gradient[None])


def solution(mesh):
    in_specs = (
        P("pipe", "dp", None, None, "mp"),
        P("pipe", "dp", None, "mp"),
        P("pipe", "mp"),
        P("pipe", "mp", None),
        P("pipe", "dp", None, None),
        P("pipe", "dp", None, None, None),
        P(),
        P(),
        P(),
    )
    out_specs = (P("pipe", "dp", None, None, "mp"), P("pipe", ("mp", "dp"), None))
    return jax.shard_map(
        per_device, mesh=mesh, in_specs=in_specs, out_specs=out_specs, check_vma=False
    )
```

profile of v0, /device:TPU:1, one launch (start us, length us, event | category | flops | bytes accessed | tf_op | source)
XLA Modules:
  0.0 552.8 jit_solution(7650471766147004055)
XLA Ops:
  7.2 1.4 fusion.17
  9.3 1.7 select_bitcast_fusion
  11.1 0.9 dynamic-slice_reduce_fusion
  12.0 1.3 dynamic_slice.15
  13.3 0.6 iota_compare_fusion
  14.0 295.9 %all-reduce.4.cloned.1.call-done = bf16[10,64,2048]{2,1,0:T(8,128)(2,1)} async-done(((bf16[10,64,2048]{2,1,0:T(8,128)(2,1)}), bf16[10,64,2048]{2,1,0:T(8,128)(2,1)}) %all-reduce.4.cloned.1.call-update) | async-done | bytes 2621456 | tf_op jit(solution)/shard_map/psum | solution.py:14
  309.9 2.3 gather_fusion
  312.2 0.9 broadcast_select_fusion
  313.1 9.1 %collective-permute-start = (bf16[2,64,2048]{2,1,0:T(8,128)(2,1)}, bf16[2,64,2048]{2,1,0:T(8,128)(2,1)S(1)}, u32[]{:S(2)}, u32[]{:S(2)}) collective-permute-start(bf16[2,64,2048]{2,1,0:T(8,128)(2,1)} %broadcast_select_fusion), channel_id=1, source_target_pairs={{0,4},{4,8},{8,12},{12,16},{16,20},{20,24},{24,28},{28,32},{32,36}... | collective-permute-start | bytes 1572872 | tf_op jit(solution)/shard_map/ppermute | solution.py:20
  322.9 0.2 fusion.8
  323.1 5.6 %collective-permute-done = bf16[2,64,2048]{2,1,0:T(8,128)(2,1)S(1)} collective-permute-done((bf16[2,64,2048]{2,1,0:T(8,128)(2,1)}, bf16[2,64,2048]{2,1,0:T(8,128)(2,1)S(1)}, u32[]{:S(2)}, u32[]{:S(2)}) %collective-permute-start) | collective-permute-done | bytes 524320 | tf_op jit(solution)/shard_map/ppermute | solution.py:20
  328.6 0.8 copy-done.2
  329.4 1.3 fusion.6
  330.8 9.3 %all-reduce = (bf16[128]{0:T(256)(128)(2,1)S(1)}, bf16[128]{0:T(256)(128)(2,1)S(1)}) all-reduce(bf16[128]{0:T(256)(128)(2,1)S(1)} %convert_element_type.85, bf16[128]{0:T(256)(128)(2,1)S(1)} %fusion.8), channel_id=1, replica_groups=mesh['dp'=16,'pipe'=16,'mp'=4] {'mp'}, use_global_device_ids=true, to_apply=%region_3.4 | all-reduce | flops 256 | bytes 1024 | tf_op jit(solution)/shard_map/psum | solution.py:56
  340.2 1.1 fusion.2
  341.4 0.8 fusion.10
  342.3 2.1 add_convert_fusion
  344.4 62.2 %all-reduce.6.cloned.1.call-done = bf16[128,512]{1,0:T(8,128)(2,1)} async-done(((bf16[128,512]{1,0:T(8,128)(2,1)}), bf16[128,512]{1,0:T(8,128)(2,1)}) %all-reduce.6.cloned.1.call-update) | async-done | bytes 131088 | tf_op jit(solution)/shard_map/psum | solution.py:55
  406.6 0.8 multiply_convert_fusion.2
  407.4 3.8 collective-permute-start.1
  411.3 1.0 collective-permute-done.1
  412.3 131.7 %reduce-scatter.2.cloned.1.call-done = bf16[128,512]{1,0:T(8,128)(2,1)} async-done(((bf16[2048,512]{1,0:T(8,128)(2,1)}), bf16[128,512]{1,0:T(8,128)(2,1)}) %reduce-scatter.2.cloned.1.call-update) | async-done | bytes 131088 | tf_op jit(solution)/shard_map/reduce_scatter | solution.py:79
  544.0 1.6 bitcast_convert_fusion
  545.6 0.6 copy.14
  (25 shorter events, 0.5 us)
Async XLA Ops:
  7.2 333.0 %copy-start = (bf16[1,2048,512]{2,1,0:T(8,128)(2,1)S(1)}, bf16[1,2048,512]{2,1,0:T(8,128)(2,1)}, u32[]{:S(2)}) copy-start(bf16[1,2048,512]{2,1,0:T(8,128)(2,1)} %param.12) | copy-start | bytes 6291460
  7.2 302.7 %all-reduce.4.cloned.1.call-start = ((), (), s32[]{:S(2)}) async-start(), calls=%async_computation.1 | async-start | bytes 5242880 | tf_op jit(solution)/shard_map/psum | solution.py:14
  11.0 311.2 %copy-start.5 = (bf16[1,2048]{1,0:T(2,128)(2,1)S(1)}, bf16[1,2048]{1,0:T(2,128)(2,1)}, u32[]{:S(2)}) copy-start(bf16[1,2048]{1,0:T(2,128)(2,1)} %param.11) | copy-start | bytes 12292
  11.0 311.9 %copy-start.1 = (bf16[1,1,128,2048]{3,2,1,0:T(8,128)(2,1)S(1)}, bf16[1,1,128,2048]{3,2,1,0:T(8,128)(2,1)}, u32[]{:S(2)}) copy-start(bf16[1,1,128,2048]{3,2,1,0:T(8,128)(2,1)} %param.10) | copy-start | bytes 1572868
  11.0 395.5 %all-reduce.6.cloned.1.call-start = ((), (), s32[]{:S(2)}) async-start(), calls=%async_computation.2 | async-start | bytes 262144 | tf_op jit(solution)/shard_map/psum | solution.py:55
  312.2 29.2 %copy-start.3 = (bf16[1,1,128,512]{3,2,1,0:T(8,128)(2,1)S(1)}, bf16[1,1,128,512]{3,2,1,0:T(8,128)(2,1)}, u32[]{:S(2)}) copy-start(bf16[1,1,128,512]{3,2,1,0:T(8,128)(2,1)} %param.13) | copy-start | bytes 393220
  313.1 15.5 %collective-permute-start = (bf16[2,64,2048]{2,1,0:T(8,128)(2,1)}, bf16[2,64,2048]{2,1,0:T(8,128)(2,1)S(1)}, u32[]{:S(2)}, u32[]{:S(2)}) collective-permute-start(bf16[2,64,2048]{2,1,0:T(8,128)(2,1)} %broadcast_select_fusion), channel_id=1, source_target_pairs={{0,4},{4,8},{8,12},{12,16},{16,20},{20,24},{24,28},{28,32},{32,36}... | collective-permute-start | bytes 1572872 | tf_op jit(solution)/shard_map/ppermute | solution.py:20
  328.6 0.8 copy-start.2
  341.3 0.9 copy-start.4
  341.3 202.7 %reduce-scatter.2.cloned.1.call-start = ((), (), s32[]{:S(2)}) async-start(), calls=%async_computation.3 | async-start | bytes 2228224 | tf_op jit(solution)/shard_map/reduce_scatter | solution.py:79
  407.4 4.9 collective-permute-start.1
Sparse Core Ops, SparseCore 0:
  11.5 298.2 all-reduce.3
  341.4 65.1 all-reduce.5
  412.7 131.2 reduce-scatter.1
where the time goes:
time: 553 us
  waiting for transfers between devices  496 us (90%)
  between operations  15.2 us (3%)
  starting transfers between devices  13.1 us (2%)
  blocking collectives  9.26 us (2%)
  local copies, waits for them, and re-layouts  7.54 us (1%)
  other arithmetic  7.31 us (1%)
    psum x1, waiting for transfers between devices, from_root(): return lax.psum(kept, axis)  296 us
    reduce_scatter x1, waiting for transfers between devices, per_device(): lax.psum_scatter((replay_part + own_part).astype(jnp.bfloat16), 'dp', sca...  132 us
    psum x1, waiting for transfers between devices, per_device(): lax.psum(partial_keys.astype(jnp.bfloat16), 'mp').astype(jnp.float32)  62.2 us
    ppermute x2, starting transfers between devices, from_behind(): return lax.ppermute(value, axis, pairs)  12.9 us
  transfers between devices with their start and end apart: 5, of which 5 were waited for; matrix products, arithmetic and copies ran while one was open for 1% of the time, Pallas kernels for 0%

commit v1 on v0

v1 whole, which is shorter than its diff:
```python
import functools
import jax
import jax.numpy as jnp
from jax import lax
from jax.experimental import pallas as pl
from jax.experimental.pallas import tpu as pltpu
from jax.sharding import PartitionSpec as P

MESH = pl.DeviceIdType.MESH
XN = 4
ZN = 4
EPS = 1e-05
F32 = jnp.float32
BF16 = jnp.bfloat16


def diagonal(rows, columns):
    return lax.broadcasted_iota(jnp.int32, (rows, columns), 0) == lax.broadcasted_iota(
        jnp.int32, (rows, columns), 1
    )


def to_row(column, columns):
    rows = column.shape[0]
    return jnp.sum(jnp.where(diagonal(rows, columns), column, 0.0), axis=0, keepdims=True)


def to_column(row, rows):
    return jnp.sum(jnp.where(diagonal(rows, row.shape[1]), row, 0.0), axis=1, keepdims=True)


class Copies:
    def __init__(self, send, recv):
        self.send, self.recv, self.count, self.started = send, recv, 0, []

    def start(self, source, target, device):
        copy = pltpu.make_async_remote_copy(
            src_ref=source,
            dst_ref=target,
            send_sem=self.send.at[self.count],
            recv_sem=self.recv.at[self.count],
            device_id=device,
            device_id_type=MESH,
        )
        self.count += 1
        copy.start()
        self.started.append(copy)
        return copy

    def finish(self):
        for copy in self.started:
            copy.wait_send()


def kernel(
    width_total,
    failed,
    counts,
    table,
    stash,
    own_input,
    gain,
    weight,
    own_cotangent,
    replay_cotangent,
    keys_out,
    grad_out,
    cand_p,
    cand_n,
    cand_a,
    cand_b,
    chosen,
    arrived,
    own_in,
    weight_in,
    cot_parts,
    cot_x,
    cot_sum,
    cot_z,
    cot_all,
    own_sum,
    own_sums,
    replay_sum,
    replay_sums,
    mixed,
    back,
    key_parts,
    key_got,
    key_all,
    key_pick,
    key_z,
    key_last,
    key_in,
    grad_parts,
    grad_x,
    grad_half,
    grad_z,
    local_sem,
    send_sem,
    recv_sem,
):
    section = lax.axis_index("pipe")
    replica = lax.axis_index("dp")
    m = lax.axis_index("mp")
    sections = lax.axis_size("pipe")
    widths = lax.axis_size("mp")
    x = lax.rem(replica, XN)
    z = replica // XN
    half, features = stash.shape[1:]
    chunk = 2 * half
    own_rows = own_input.shape[0]
    key_width = weight.shape[1]
    share = key_width // widths
    block = features // (XN * ZN)
    upcoming = lax.rem(section + 1, sections)
    previous = lax.rem(section + sections - 1, sections)

    def x_peer(k):
        return {"dp": z * XN + lax.rem(x + k, XN)}

    def z_peer(k):
        return {"dp": lax.rem(z + k, ZN) * XN + x}

    def m_peer(k):
        return {"mp": lax.rem(m + k, widths)}

    loads = []

    def load(source, target):
        copy = pltpu.make_async_copy(source, target, local_sem.at[len(loads)])
        copy.start()
        loads.append(copy)
        return copy

    load_own = load(own_input, own_in)
    load_p = load(stash.at[2 * lax.rem(x + 1, XN)], cand_p.at[0])
    load_n = load(stash.at[2 * lax.rem(x + 3, XN) + 1], cand_n.at[0])
    load_a = load(stash.at[2 * x], cand_a.at[0])
    load_b = load(stash.at[2 * x + 1], cand_b.at[0])
    load_w = load(weight, weight_in)

    barrier = pltpu.get_barrier_semaphore()
    peers = [x_peer(k) for k in range(1, XN)]
    peers += [z_peer(k) for k in range(1, ZN)]
    peers += [m_peer(k) for k in range(1, widths)]
    peers += [{"pipe": upcoming}, {"pipe": previous}]
    for peer in peers:
        pl.semaphore_signal(barrier, inc=1, device_id=peer, device_id_type=MESH)
    pl.semaphore_wait(barrier, len(peers))

    copies = Copies(send_sem, recv_sem)

    far = 2 * lax.rem(x + 2, XN)
    far_p = copies.start(stash.at[far], cand_p.at[1], x_peer(1))
    far_n = copies.start(stash.at[far + 1], cand_n.at[1], x_peer(3))
    near_b = copies.start(stash.at[2 * lax.rem(x + 1, XN) + 1], cand_b.at[1], x_peer(1))
    near_a = copies.start(stash.at[2 * lax.rem(x + 3, XN)], cand_a.at[1], x_peer(3))

    quarter = pl.ds(pl.multiple_of(m * share, 128), share)
    slot_total = 2
    token_total = replay_cotangent.shape[0] // slot_total
    batches = 4 * chunk // token_total
    live = counts[section, replica]
    cot = replay_cotangent[:, quarter].astype(F32)
    for batch in range(batches):
        value = None
        for j in range(slot_total):
            hit = jnp.logical_and(table[section, 2 * replica + j] == batch, live > j)
            term = cot[j * token_total : (j + 1) * token_total] * hit.astype(F32)
            value = term if value is None else value + term
        cot_parts[batch * token_total : (batch + 1) * token_total] = value.astype(BF16)

    def rows_of(place):
        return pl.ds(pl.multiple_of(place * chunk, 16), chunk)

    cot_copies = [
        copies.start(cot_parts.at[rows_of(lax.rem(x + k, XN))], cot_x.at[k - 1], x_peer(k))
        for k in range(1, XN)
    ]

    scaling = gain[...].astype(F32)
    load_own.wait()
    own_float = own_in[...].astype(F32)
    mixed[:own_rows] = (own_float * scaling).astype(BF16)
    column = jnp.sum(own_float * own_float, axis=1, keepdims=True)
    own_sum[...] = jnp.broadcast_to(to_row(column, own_rows), own_sum.shape)
    own_copies = [
        copies.start(own_sum, own_sums.at[k - 1], m_peer(k)) for k in range(1, widths)
    ]

    value = cot_parts[rows_of(x)].astype(F32)
    for k, copy in enumerate(cot_copies):
        copy.wait_recv()
        value = value + cot_x[k].astype(F32)
    cot_sum[...] = value.astype(BF16)
    cot_copies = [copies.start(cot_sum, cot_z.at[k - 1], z_peer(k)) for k in range(1, ZN)]

    total = own_sum[...]
    for k, copy in enumerate(own_copies):
        copy.wait_recv()
        total = total + own_sums[k]
    factor = lax.rsqrt(total / width_total + EPS)
    keeper = (replica != failed[section]).astype(F32)
    column = to_column(factor[:1], own_rows) * keeper
    back[:own_rows] = (own_cotangent[...].astype(F32) * column).astype(BF16)

    source = lax.rem(failed[upcoming], XN)
    load_p.wait()
    far_p.wait_recv()
    cand_p[2] = jnp.where(source == lax.rem(x + 3, XN), cand_p[1], cand_p[0])
    pass_p = copies.start(cand_p.at[2], cand_a.at[2], x_peer(1))
    load_n.wait()
    far_n.wait_recv()
    cand_n[2] = jnp.where(source == lax.rem(x + 1, XN), cand_n[1], cand_n[0])
    pass_n = copies.start(cand_n.at[2], cand_b.at[2], x_peer(3))

    value = cot_sum[...].astype(F32)
    for k, copy in enumerate(cot_copies):
        copy.wait_recv()
        value = value + cot_z[k].astype(F32)
    cot_all[m] = value.astype(BF16)
    cot_copies = [
        copies.start(cot_all.at[m], cot_all.at[m], m_peer(k)) for k in range(1, widths)
    ]

    here = source == x
    load_a.wait()
    near_a.wait_recv()
    pass_p.wait_recv()
    one = jnp.where(source == lax.rem(x + 1, XN), cand_a[1], cand_a[2])
    chosen[0] = jnp.where(here, cand_a[0], one)
    ahead = [copies.start(chosen.at[0], arrived.at[0], {"pipe": upcoming})]
    load_b.wait()
    near_b.wait_recv()
    pass_n.wait_recv()
    one = jnp.where(source == lax.rem(x + 3, XN), cand_b[1], cand_b[2])
    chosen[1] = jnp.where(here, cand_b[0], one)
    ahead += [copies.start(chosen.at[1], arrived.at[1], {"pipe": upcoming})]

    for copy in cot_copies:
        copy.wait_recv()
    load_w.wait()

    valid = (failed[section] // XN == z).astype(F32)
    masked = scaling * valid
    columns = []
    for part in range(2):
        ahead[part].wait_recv()
        rows = slice(own_rows + part * half, own_rows + (part + 1) * half)
        value = arrived[part].astype(F32)
        mixed[rows] = (value * masked).astype(BF16)
        columns.append(jnp.sum(value * value, axis=1, keepdims=True))
    padded = replay_sum.shape[1]
    row = to_row(jnp.concatenate(columns, axis=0), padded)
    replay_sum[...] = jnp.broadcast_to(row, replay_sum.shape)
    sum_copies = [
        copies.start(replay_sum, replay_sums.at[k - 1], m_peer(k)) for k in range(1, widths)
    ]
    partial = jnp.dot(mixed[own_rows:], weight_in[...], preferred_element_type=F32)
    for place in range(widths):
        key_parts[place] = partial[:, place * share : (place + 1) * share].astype(BF16)
    key_copies = [
        copies.start(key_parts.at[lax.rem(m + k, widths)], key_got.at[k - 1], m_peer(k))
        for k in range(1, widths)
    ]

    total = replay_sum[...]
    for k, copy in enumerate(sum_copies):
        copy.wait_recv()
        total = total + replay_sums[k]
    factor = lax.rsqrt(total / width_total + EPS)
    column = to_column(factor[:1], chunk)
    for place in range(widths):
        value = cot_all[place].astype(F32) * column
        back[own_rows:, place * share : (place + 1) * share] = value.astype(BF16)

    contract = (((0,), (0,)), ((), ()))
    group = XN * block
    grad_copies = []
    for step in range(ZN):
        place = lax.rem(z + 1 + step, ZN)
        window = pl.ds(pl.multiple_of(place * group, 128), group)
        product = lax.dot_general(
            mixed[:, window], back[...], contract, preferred_element_type=F32
        ).astype(BF16)
        for k in range(XN):
            grad_parts[step, k] = product[k * block : (k + 1) * block]
        grad_copies.append(
            [
                copies.start(
                    grad_parts.at[step, lax.rem(x + k, XN)], grad_x.at[step, k - 1], x_peer(k)
                )
                for k in range(1, XN)
            ]
        )

    value = key_parts[m].astype(F32)
    for k, copy in enumerate(key_copies):
        copy.wait_recv()
        value = value + key_got[k].astype(F32)
    key_all[rows_of(x)] = (value * column).astype(BF16)
    key_copies = [
        copies.start(key_all.at[rows_of(x)], key_all.at[rows_of(x)], x_peer(k))
        for k in range(1, XN)
    ]

    last = []
    for step in range(ZN):
        value = grad_parts[step, x].astype(F32)
        for k, copy in enumerate(grad_copies[step]):
            copy.wait_recv()
            value = value + grad_x[step, k].astype(F32)
        if step < ZN - 1:
            grad_half[step] = value.astype(BF16)
            last.append(copies.start(grad_half.at[step], grad_z.at[step], z_peer(step + 1)))
        else:
            grad_out[...] = value
        if step == 0:
            for copy in key_copies:
                copy.wait_recv()
            key_last_copies = []
            for k in range(ZN):
                there = lax.rem(z + k, ZN) * XN + x
                for j in range(slot_total):
                    named = table[section, 2 * there + j]
                    kept = counts[section, there] > j
                    value = None
                    for batch in range(batches):
                        rows = slice(batch * token_total, (batch + 1) * token_total)
                        hit = jnp.logical_and(named == batch, kept).astype(F32)
                        term = key_all[rows].astype(F32) * hit
                        value = term if value is None else value + term
                    key_pick[k, j * token_total : (j + 1) * token_total] = value.astype(BF16)
                if k > 0:
                    key_last_copies.append(
                        copies.start(key_pick.at[k], key_z.at[k - 1], z_peer(k))
                    )

    value = key_pick[0].astype(F32)
    for k, copy in enumerate(key_last_copies):
        copy.wait_recv()
        value = value + key_z[k].astype(F32)
    key_last[...] = value.astype(BF16)
    final = copies.start(key_last, key_in, {"pipe": upcoming})

    value = grad_out[...]
    for k, copy in enumerate(last):
        copy.wait_recv()
        value = value + grad_z[k].astype(F32)
    grad_out[...] = value
    final.wait_recv()
    keys_out[...] = key_in[...]
    copies.finish()


def per_device(
    stash, own_input, gain, key_weight, own_cotangent, replay_cotangent, failed, counts, table
):
    widths = lax.axis_size("mp")
    batches, tokens, features = stash.shape[2:]
    half = batches * tokens // (2 * XN)
    chunk = 2 * half
    own_rows = own_input.shape[2]
    key_width = key_weight.shape[2]
    share = key_width // widths
    slots = replay_cotangent.shape[2]
    replay_rows = slots * tokens
    block = features // (XN * ZN)
    others = max(widths - 1, 1)
    padded = -(-chunk // 128) * 128
    remote = 4 + 3 + 3 + 3 + 3 * (widths - 1) + 2 + (widths - 1) + 4 * 3 + 3 + 3 + 3 + 1 + 2
    vmem = pl.BlockSpec(memory_space=pltpu.VMEM)
    smem = pl.BlockSpec(memory_space=pltpu.SMEM)
    whole = pl.BlockSpec(memory_space=pl.ANY)
    keys, gradient = pl.pallas_call(
        functools.partial(kernel, features * widths),
        out_shape=(
            jax.ShapeDtypeStruct((replay_rows, share), BF16),
            jax.ShapeDtypeStruct((block, key_width), F32),
        ),
        in_specs=[smem, smem, smem, whole, whole, vmem, whole, vmem, vmem],
        out_specs=(vmem, vmem),
        scratch_shapes=[
            pltpu.VMEM((3, half, features), BF16),
            pltpu.VMEM((3, half, features), BF16),
            pltpu.VMEM((3, half, features), BF16),
            pltpu.VMEM((3, half, features), BF16),
            pltpu.VMEM((2, half, features), BF16),
            pltpu.VMEM((2, half, features), BF16),
            pltpu.VMEM((own_rows, features), BF16),
            pltpu.VMEM((features, key_width), BF16),
            pltpu.VMEM((4 * chunk, share), BF16),
            pltpu.VMEM((XN - 1, chunk, share), BF16),
            pltpu.VMEM((chunk, share), BF16),
            pltpu.VMEM((ZN - 1, chunk, share), BF16),
            pltpu.VMEM((widths, chunk, share), BF16),
            pltpu.VMEM((8, own_rows), F32),
            pltpu.VMEM((others, 8, own_rows), F32),
            pltpu.VMEM((8, padded), F32),
            pltpu.VMEM((others, 8, padded), F32),
            pltpu.VMEM((own_rows + chunk, features), BF16),
            pltpu.VMEM((own_rows + chunk, key_width), BF16),
            pltpu.VMEM((widths, chunk, share), BF16),
            pltpu.VMEM((others, chunk, share), BF16),
            pltpu.VMEM((4 * chunk, share), BF16),
            pltpu.VMEM((ZN, replay_rows, share), BF16),
            pltpu.VMEM((ZN - 1, replay_rows, share), BF16),
            pltpu.VMEM((replay_rows, share), BF16),
            pltpu.VMEM((replay_rows, share), BF16),
            pltpu.VMEM((ZN, XN, block, key_width), BF16),
            pltpu.VMEM((ZN, XN - 1, block, key_width), BF16),
            pltpu.VMEM((ZN - 1, block, key_width), BF16),
            pltpu.VMEM((ZN - 1, block, key_width), BF16),
            pltpu.SemaphoreType.DMA((6,)),
            pltpu.SemaphoreType.DMA((remote,)),
            pltpu.SemaphoreType.DMA((remote,)),
        ],
        compiler_params=pltpu.CompilerParams(
            collective_id=0, has_side_effects=True, vmem_limit_bytes=48 * 1024 * 1024
        ),
    )(
        failed,
        counts,
        table.reshape(table.shape[0], -1),
        stash.reshape(2 * XN, half, features),
        own_input.reshape(own_rows, features),
        gain,
        key_weight.reshape(features, key_width),
        own_cotangent.reshape(own_rows, key_width),
        replay_cotangent.reshape(replay_rows, key_width),
    )
    return (keys.reshape(1, 1, slots, tokens, share), gradient[None])


def solution(mesh):
    in_specs = (
        P("pipe", "dp", None, None, "mp"),
        P("pipe", "dp", None, "mp"),
        P("pipe", "mp"),
        P("pipe", "mp", None),
        P("pipe", "dp", None, None),
        P("pipe", "dp", None, None, None),
        P(),
        P(),
        P(),
    )
    out_specs = (P("pipe", "dp", None, None, "mp"), P("pipe", ("mp", "dp"), None))
    return jax.shard_map(
        per_device, mesh=mesh, in_specs=in_specs, out_specs=out_specs, check_vma=False
    )
```

time: 553 us -> 123 us (0.22)
  the two profiles are of different devices: /device:TPU:1 before, /device:TPU:12 now
where the time goes in v1:
time: 123 us; the launch traced here: 122 us
  Pallas kernels  111 us (90%)
  local copies, waits for them, and re-layouts  10.4 us (8%)
    pallas_call x1, Pallas kernels, per_device(): pl.pallas_call(functools.partial(kernel, features * widths), out_shape=(j...  111 us
    unnamed x19, local copies, waits for them, and re-layouts  10.3 us

profile of v1, /device:TPU:12, one launch (start us, length us, event | category | flops | bytes accessed | tf_op | source)
XLA Modules:
  0.0 122.5 jit_solution(9933348217396511228)
XLA Ops:
  0.6 0.8 copy.12
  1.4 0.1 copy.13.table
  1.5 0.0 copy-start
  1.5 1.7 %copy-done = bf16[1,1,10,64,2048]{4,3,2,1,0:T(8,128)(2,1)S(1)} copy-done((bf16[1,1,10,64,2048]{4,3,2,1,0:T(8,128)(2,1)S(1)}, bf16[1,1,10,64,2048]{4,3,2,1,0:T(8,128)(2,1)}, u32[]{:S(2)}) %copy-start) | copy-done | bytes 2621464
  3.2 0.0 copy-start.1
  3.2 1.6 %copy-done.1 = bf16[1,2048,512]{2,1,0:T(8,128)(2,1)S(1)} copy-done((bf16[1,2048,512]{2,1,0:T(8,128)(2,1)S(1)}, bf16[1,2048,512]{2,1,0:T(8,128)(2,1)}, u32[]{:S(2)}) %copy-start.1) | copy-done | bytes 2097176
  4.8 0.0 copy-start.2
  4.8 1.0 copy-done.2
  5.9 0.0 copy-start.3
  5.9 0.9 copy-done.3
  6.8 0.0 copy-start.4
  6.8 0.9 copy-done.4
  7.7 0.0 copy-start.5
  7.7 0.7 copy-done.5
  8.4 0.0 copy-start.6
  8.4 0.7 copy-done.6
  9.1 0.0 copy-start.7
  9.1 0.7 copy-done.7
  9.7 111.4 %shard_map.104 = (bf16[128,128]{1,0:T(8,128)(2,1)S(1)}, f32[128,512]{1,0:T(8,128)S(1)}) custom-call(s32[16]{0:T(128)S(1)} %copy-done.7, s32[16,16]{1,0:T(8,128)S(1)} %copy-done.5, s32[16,32]{1,0:T(8,128)S(1)} %copy.13.table, bf16[8,80,2048]{2,1,0:T(8,128)(2,1)S(1)} %bitcast.8, bf16[128,2048]{1,0:T(8,128)(2,1)S(1)} %bitcast.10, ...), custom_call_target="tpu_custom_call" | custom-call | tf_op jit(solution)/shard_map/pallas_call | solution.py:375
  121.2 0.6 copy.16
  121.8 0.7 copy.17
Async XLA Ops:
  1.5 1.7 %copy-start = (bf16[1,1,10,64,2048]{4,3,2,1,0:T(8,128)(2,1)S(1)}, bf16[1,1,10,64,2048]{4,3,2,1,0:T(8,128)(2,1)}, u32[]{:S(2)}) copy-start(bf16[1,1,10,64,2048]{4,3,2,1,0:T(8,128)(2,1)} %param.9) | copy-start | bytes 7864324
  3.2 1.6 %copy-start.1 = (bf16[1,2048,512]{2,1,0:T(8,128)(2,1)S(1)}, bf16[1,2048,512]{2,1,0:T(8,128)(2,1)}, u32[]{:S(2)}) copy-start(bf16[1,2048,512]{2,1,0:T(8,128)(2,1)} %param.12) | copy-start | bytes 6291460
  4.8 1.0 copy-start.2
  5.9 0.9 copy-start.3
  6.8 0.9 copy-start.4
  7.7 0.7 copy-start.5
  8.4 0.7 copy-start.6
  9.1 0.7 copy-start.7

commit v2 on v1

--- a/solution.py
+++ b/solution.py
@@ -9,6 +9,7 @@
 MESH = pl.DeviceIdType.MESH
 XN = 4
 ZN = 4
+PIECES = 2
 EPS = 1e-05
 F32 = jnp.float32
 BF16 = jnp.bfloat16
@@ -54,17 +55,23 @@
 
 def kernel(
     width_total,
-    failed,
-    counts,
-    table,
+    failed_hbm,
+    counts_hbm,
+    table_hbm,
     stash,
     own_input,
-    gain,
+    gain_hbm,
     weight,
     own_cotangent,
     replay_cotangent,
     keys_out,
     grad_out,
+    failed,
+    counts,
+    table,
+    gain,
+    own_cot,
+    replay_cot,
     cand_p,
     cand_n,
     cand_a,
@@ -92,9 +99,13 @@
     key_last,
     key_in,
     grad_parts,
+    grad_far,
+    grad_pass,
     grad_x,
-    grad_half,
-    grad_z,
+    half_far,
+    half_got,
+    half_send,
+    half_z,
     local_sem,
     send_sem,
     recv_sem,
@@ -124,21 +135,6 @@
     def m_peer(k):
         return {"mp": lax.rem(m + k, widths)}
 
-    loads = []
-
-    def load(source, target):
-        copy = pltpu.make_async_copy(source, target, local_sem.at[len(loads)])
-        copy.start()
-        loads.append(copy)
-        return copy
-
-    load_own = load(own_input, own_in)
-    load_p = load(stash.at[2 * lax.rem(x + 1, XN)], cand_p.at[0])
-    load_n = load(stash.at[2 * lax.rem(x + 3, XN) + 1], cand_n.at[0])
-    load_a = load(stash.at[2 * x], cand_a.at[0])
-    load_b = load(stash.at[2 * x + 1], cand_b.at[0])
-    load_w = load(weight, weight_in)
-
     barrier = pltpu.get_barrier_semaphore()
     peers = [x_peer(k) for k in range(1, XN)]
     peers += [z_peer(k) for k in range(1, ZN)]
@@ -146,26 +142,41 @@
     peers += [{"pipe": upcoming}, {"pipe": previous}]
     for peer in peers:
         pl.semaphore_signal(barrier, inc=1, device_id=peer, device_id_type=MESH)
-    pl.semaphore_wait(barrier, len(peers))
-
-    copies = Copies(send_sem, recv_sem)
-
-    far = 2 * lax.rem(x + 2, XN)
-    far_p = copies.start(stash.at[far], cand_p.at[1], x_peer(1))
-    far_n = copies.start(stash.at[far + 1], cand_n.at[1], x_peer(3))
-    near_b = copies.start(stash.at[2 * lax.rem(x + 1, XN) + 1], cand_b.at[1], x_peer(1))
-    near_a = copies.start(stash.at[2 * lax.rem(x + 3, XN)], cand_a.at[1], x_peer(3))
+
+    loads = []
+
+    def load(source, target):
+        copy = pltpu.make_async_copy(source, target, local_sem.at[len(loads)])
+        copy.start()
+        loads.append(copy)
+        return copy
+
+    load_counts = load(counts_hbm, counts)
+    load_table = load(table_hbm, table)
+    load_failed = load(failed_hbm, failed)
+    load_replay = load(replay_cotangent, replay_cot)
+    load_gain = load(gain_hbm, gain)
+    load_own = load(own_input, own_in)
+    load_cot = load(own_cotangent, own_cot)
+    load_p = load(stash.at[2 * lax.rem(x + 1, XN)], cand_p.at[0])
+    load_n = load(stash.at[2 * lax.rem(x + 3, XN) + 1], cand_n.at[0])
+    load_a = load(stash.at[2 * x], cand_a.at[0])
+    load_b = load(stash.at[2 * x + 1], cand_b.at[0])
+    load_w = load(weight, weight_in)
 
     quarter = pl.ds(pl.multiple_of(m * share, 128), share)
     slot_total = 2
     token_total = replay_cotangent.shape[0] // slot_total
     batches = 4 * chunk // token_total
+    load_counts.wait()
+    load_table.wait()
+    load_replay.wait()
     live = counts[section, replica]
-    cot = replay_cotangent[:, quarter].astype(F32)
+    cot = replay_cot[:, quarter].astype(F32)
     for batch in range(batches):
         value = None
         for j in range(slot_total):
-            hit = jnp.logical_and(table[section, 2 * replica + j] == batch, live > j)
+            hit = jnp.logical_and(table[section, j, replica] == batch, live > j)
             term = cot[j * token_total : (j + 1) * token_total] * hit.astype(F32)
             value = term if value is None else value + term
         cot_parts[batch * token_total : (batch + 1) * token_total] = value.astype(BF16)
@@ -173,11 +184,25 @@
     def rows_of(place):
         return pl.ds(pl.multiple_of(place * chunk, 16), chunk)
 
+    pl.semaphore_wait(barrier, len(peers))
+    copies = Copies(send_sem, recv_sem)
     cot_copies = [
         copies.start(cot_parts.at[rows_of(lax.rem(x + k, XN))], cot_x.at[k - 1], x_peer(k))
         for k in range(1, XN)
     ]
 
+    far = 2 * lax.rem(x + 2, XN)
+    windows = [slice(c * features // PIECES, (c + 1) * features // PIECES) for c in range(PIECES)]
+    far_p, far_n, near_a, near_b = [], [], [], []
+    for w in windows:
+        far_p.append(copies.start(stash.at[far, :, w], cand_p.at[1, :, w], x_peer(1)))
+        far_n.append(copies.start(stash.at[far + 1, :, w], cand_n.at[1, :, w], x_peer(3)))
+        near = 2 * lax.rem(x + 1, XN) + 1
+        near_b.append(copies.start(stash.at[near, :, w], cand_b.at[1, :, w], x_peer(1)))
+        near = 2 * lax.rem(x + 3, XN)
+        near_a.append(copies.start(stash.at[near, :, w], cand_a.at[1, :, w], x_peer(3)))
+
+    load_gain.wait()
     scaling = gain[...].astype(F32)
     load_own.wait()
     own_float = own_in[...].astype(F32)
@@ -200,20 +225,45 @@
         copy.wait_recv()
         total = total + own_sums[k]
     factor = lax.rsqrt(total / width_total + EPS)
+    load_failed.wait()
+    load_cot.wait()
     keeper = (replica != failed[section]).astype(F32)
     column = to_column(factor[:1], own_rows) * keeper
-    back[:own_rows] = (own_cotangent[...].astype(F32) * column).astype(BF16)
+    back[:own_rows] = (own_cot[...].astype(F32) * column).astype(BF16)
 
     source = lax.rem(failed[upcoming], XN)
+    here = source == x
+    before = source == lax.rem(x + 3, XN)
+    after = source == lax.rem(x + 1, XN)
     load_p.wait()
-    far_p.wait_recv()
-    cand_p[2] = jnp.where(source == lax.rem(x + 3, XN), cand_p[1], cand_p[0])
-    pass_p = copies.start(cand_p.at[2], cand_a.at[2], x_peer(1))
     load_n.wait()
-    far_n.wait_recv()
-    cand_n[2] = jnp.where(source == lax.rem(x + 1, XN), cand_n[1], cand_n[0])
-    pass_n = copies.start(cand_n.at[2], cand_b.at[2], x_peer(3))
-
+    pass_p, pass_n = [], []
+
+    def relay(c):
+        w = windows[c]
+        far_p[c].wait_recv()
+        cand_p[2, :, w] = jnp.where(before, cand_p[1, :, w], cand_p[0, :, w])
+        pass_p.append(copies.start(cand_p.at[2, :, w], cand_a.at[2, :, w], x_peer(1)))
+        far_n[c].wait_recv()
+        cand_n[2, :, w] = jnp.where(after, cand_n[1, :, w], cand_n[0, :, w])
+        pass_n.append(copies.start(cand_n.at[2, :, w], cand_b.at[2, :, w], x_peer(3)))
+
+    ahead = []
+
+    def choose(c):
+        w = windows[c]
+        near_a[c].wait_recv()
+        pass_p[c].wait_recv()
+        one = jnp.where(after, cand_a[1, :, w], cand_a[2, :, w])
+        chosen[0, :, w] = jnp.where(here, cand_a[0, :, w], one)
+        ahead.append(copies.start(chosen.at[0, :, w], arrived.at[0, :, w], {"pipe": upcoming}))
+        near_b[c].wait_recv()
+        pass_n[c].wait_recv()
+        one = jnp.where(before, cand_b[1, :, w], cand_b[2, :, w])
+        chosen[1, :, w] = jnp.where(here, cand_b[0, :, w], one)
+        ahead.append(copies.start(chosen.at[1, :, w], arrived.at[1, :, w], {"pipe": upcoming}))
+
+    relay(0)
     value = cot_sum[...].astype(F32)
     for k, copy in enumerate(cot_copies):
         copy.wait_recv()
@@ -222,34 +272,29 @@
     cot_copies = [
         copies.start(cot_all.at[m], cot_all.at[m], m_peer(k)) for k in range(1, widths)
     ]
-
-    here = source == x
     load_a.wait()
-    near_a.wait_recv()
-    pass_p.wait_recv()
-    one = jnp.where(source == lax.rem(x + 1, XN), cand_a[1], cand_a[2])
-    chosen[0] = jnp.where(here, cand_a[0], one)
-    ahead = [copies.start(chosen.at[0], arrived.at[0], {"pipe": upcoming})]
     load_b.wait()
-    near_b.wait_recv()
-    pass_n.wait_recv()
-    one = jnp.where(source == lax.rem(x + 3, XN), cand_b[1], cand_b[2])
-    chosen[1] = jnp.where(here, cand_b[0], one)
-    ahead += [copies.start(chosen.at[1], arrived.at[1], {"pipe": upcoming})]
-
-    for copy in cot_copies:
-        copy.wait_recv()
-    load_w.wait()
+    for c in range(1, PIECES):
+        relay(c)
+        choose(c - 1)
 
     valid = (failed[section] // XN == z).astype(F32)
     masked = scaling * valid
-    columns = []
-    for part in range(2):
-        ahead[part].wait_recv()
-        rows = slice(own_rows + part * half, own_rows + (part + 1) * half)
-        value = arrived[part].astype(F32)
-        mixed[rows] = (value * masked).astype(BF16)
-        columns.append(jnp.sum(value * value, axis=1, keepdims=True))
+    columns = [0.0, 0.0]
+
+    def take(c):
+        w = windows[c]
+        for part in range(2):
+            ahead[2 * c + part].wait_recv()
+            rows = slice(own_rows + part * half, own_rows + (part + 1) * half)
+            value = arrived[part, :, w].astype(F32)
+            mixed[rows, w] = (value * masked[:, w]).astype(BF16)
+            columns[part] = columns[part] + jnp.sum(value * value, axis=1, keepdims=True)
+
+    choose(PIECES - 1)
+    load_w.wait()
+    for c in range(PIECES):
+        take(c)
     padded = replay_sum.shape[1]
     row = to_row(jnp.concatenate(columns, axis=0), padded)
     replay_sum[...] = jnp.broadcast_to(row, replay_sum.shape)
@@ -264,6 +309,8 @@
         for k in range(1, widths)
     ]
 
+    for copy in cot_copies:
+        copy.wait_recv()
     total = replay_sum[...]
     for k, copy in enumerate(sum_copies):
         copy.wait_recv()
@@ -276,24 +323,54 @@
 
     contract = (((0,), (0,)), ((), ()))
     group = XN * block
-    grad_copies = []
-    for step in range(ZN):
-        place = lax.rem(z + 1 + step, ZN)
+    middle = block // 2
+    first, second = slice(0, middle), slice(middle, block)
+    turns = (2, 1, 3, 0)
+    straight, passing, added = [], [], []
+
+    def issue(step):
+        place = lax.rem(z + turns[step], ZN)
         window = pl.ds(pl.multiple_of(place * group, 128), group)
         product = lax.dot_general(
             mixed[:, window], back[...], contract, preferred_element_type=F32
         ).astype(BF16)
         for k in range(XN):
             grad_parts[step, k] = product[k * block : (k + 1) * block]
-        grad_copies.append(
-            [
-                copies.start(
-                    grad_parts.at[step, lax.rem(x + k, XN)], grad_x.at[step, k - 1], x_peer(k)
-                )
-                for k in range(1, XN)
-            ]
+        parts = grad_parts.at[step]
+        over = parts.at[lax.rem(x + 2, XN)]
+        passing.append(
+            (
+                copies.start(over.at[first], grad_far.at[step, 0], x_peer(1)),
+                copies.start(over.at[second], grad_far.at[step, 1], x_peer(3)),
+            )
         )
-
+        right, left = parts.at[lax.rem(x + 1, XN)], parts.at[lax.rem(x + 3, XN)]
+        straight.append(
+            (
+                copies.start(right.at[second], grad_x.at[step, 0, second], x_peer(1)),
+                copies.start(left.at[first], grad_x.at[step, 1, first], x_peer(3)),
+            )
+        )
+
+    def pass_on(step):
+        to_p, to_n = passing[step]
+        to_p.wait_recv()
+        value = grad_parts[step, lax.rem(x + 1, XN), first].astype(F32)
+        grad_pass[step, 0] = (value + grad_far[step, 0].astype(F32)).astype(BF16)
+        sent_p = copies.start(grad_pass.at[step, 0], grad_x.at[step, 0, first], x_peer(1))
+        to_n.wait_recv()
+        value = grad_parts[step, lax.rem(x + 3, XN), second].astype(F32)
+        grad_pass[step, 1] = (value + grad_far[step, 1].astype(F32)).astype(BF16)
+        sent_n = copies.start(grad_pass.at[step, 1], grad_x.at[step, 1, second], x_peer(3))
+        added.append((sent_p, sent_n))
+
+    def summed(step):
+        for copy in straight[step] + added[step]:
+            copy.wait_recv()
+        value = grad_parts[step, x].astype(F32)
+        return value + grad_x[step, 0].astype(F32) + grad_x[step, 1].astype(F32)
+
+    issue(0)
     value = key_parts[m].astype(F32)
     for k, copy in enumerate(key_copies):
         copy.wait_recv()
@@ -303,51 +380,67 @@
         copies.start(key_all.at[rows_of(x)], key_all.at[rows_of(x)], x_peer(k))
         for k in range(1, XN)
     ]
-
-    last = []
-    for step in range(ZN):
-        value = grad_parts[step, x].astype(F32)
-        for k, copy in enumerate(grad_copies[step]):
-            copy.wait_recv()
-            value = value + grad_x[step, k].astype(F32)
-        if step < ZN - 1:
-            grad_half[step] = value.astype(BF16)
-            last.append(copies.start(grad_half.at[step], grad_z.at[step], z_peer(step + 1)))
-        else:
-            grad_out[...] = value
-        if step == 0:
-            for copy in key_copies:
-                copy.wait_recv()
-            key_last_copies = []
-            for k in range(ZN):
-                there = lax.rem(z + k, ZN) * XN + x
-                for j in range(slot_total):
-                    named = table[section, 2 * there + j]
-                    kept = counts[section, there] > j
-                    value = None
-                    for batch in range(batches):
-                        rows = slice(batch * token_total, (batch + 1) * token_total)
-                        hit = jnp.logical_and(named == batch, kept).astype(F32)
-                        term = key_all[rows].astype(F32) * hit
-                        value = term if value is None else value + term
-                    key_pick[k, j * token_total : (j + 1) * token_total] = value.astype(BF16)
-                if k > 0:
-                    key_last_copies.append(
-                        copies.start(key_pick.at[k], key_z.at[k - 1], z_peer(k))
-                    )
-
+    issue(1)
+    pass_on(0)
+    issue(2)
+
+    for copy in key_copies:
+        copy.wait_recv()
+    key_copies = []
+    for k in range(ZN):
+        there = lax.rem(z + k, ZN) * XN + x
+        for j in range(slot_total):
+            named = table[section, j, there]
+            kept = counts[section, there] > j
+            value = None
+            for batch in range(batches):
+                rows = slice(batch * token_total, (batch + 1) * token_total)
+                hit = jnp.logical_and(named == batch, kept).astype(F32)
+                term = key_all[rows].astype(F32) * hit
+                value = term if value is None else value + term
+            key_pick[k, j * token_total : (j + 1) * token_total] = value.astype(BF16)
+        if k > 0:
+            key_copies.append(copies.start(key_pick.at[k], key_z.at[k - 1], z_peer(k)))
+
+    value = summed(0)
+    half_far[...] = value.astype(BF16)
+    over_p = copies.start(half_far.at[first], half_got.at[0], z_peer(1))
+    over_n = copies.start(half_far.at[second], half_got.at[1], z_peer(3))
+    pass_on(1)
+    issue(3)
+    arriving = []
+
+    value = summed(1)
+    half_send[0, second] = value[middle:].astype(BF16)
+    arriving.append(
+        copies.start(half_send.at[0, second], half_z.at[0, second], z_peer(1))
+    )
+    pass_on(2)
+    over_p.wait_recv()
+    half_send[0, first] = (value[:middle] + half_got[0].astype(F32)).astype(BF16)
+    arriving.append(copies.start(half_send.at[0, first], half_z.at[0, first], z_peer(1)))
+
+    value = summed(2)
+    half_send[1, first] = value[:middle].astype(BF16)
+    arriving.append(copies.start(half_send.at[1, first], half_z.at[1, first], z_peer(3)))
+    over_n.wait_recv()
+    half_send[1, second] = (value[middle:] + half_got[1].astype(F32)).astype(BF16)
+    arriving.append(
+        copies.start(half_send.at[1, second], half_z.at[1, second], z_peer(3))
+    )
+
+    pass_on(3)
     value = key_pick[0].astype(F32)
-    for k, copy in enumerate(key_last_copies):
+    for k, copy in enumerate(key_copies):
         copy.wait_recv()
         value = value + key_z[k].astype(F32)
     key_last[...] = value.astype(BF16)
     final = copies.start(key_last, key_in, {"pipe": upcoming})
 
-    value = grad_out[...]
-    for k, copy in enumerate(last):
-        copy.wait_recv()
-        value = value + grad_z[k].astype(F32)
-    grad_out[...] = value
+    value = summed(3)
+    for copy in arriving:
+        copy.wait_recv()
+    grad_out[...] = value + half_z[0].astype(F32) + half_z[1].astype(F32)
     final.wait_recv()
     keys_out[...] = key_in[...]
     copies.finish()
@@ -368,19 +461,24 @@
     block = features // (XN * ZN)
     others = max(widths - 1, 1)
     padded = -(-chunk // 128) * 128
-    remote = 4 + 3 + 3 + 3 + 3 * (widths - 1) + 2 + (widths - 1) + 4 * 3 + 3 + 3 + 3 + 1 + 2
+    remote = 8 * PIECES + 3 + 3 + 4 * (widths - 1) + 6 * ZN + 3 + 3 + 6 + 1
     vmem = pl.BlockSpec(memory_space=pltpu.VMEM)
-    smem = pl.BlockSpec(memory_space=pltpu.SMEM)
-    whole = pl.BlockSpec(memory_space=pl.ANY)
+    whole = pl.BlockSpec(memory_space=pltpu.HBM)
     keys, gradient = pl.pallas_call(
         functools.partial(kernel, features * widths),
         out_shape=(
             jax.ShapeDtypeStruct((replay_rows, share), BF16),
             jax.ShapeDtypeStruct((block, key_width), F32),
         ),
-        in_specs=[smem, smem, smem, whole, whole, vmem, whole, vmem, vmem],
+        in_specs=[whole] * 9,
         out_specs=(vmem, vmem),
         scratch_shapes=[
+            pltpu.SMEM(failed.shape, jnp.int32),
+            pltpu.SMEM(counts.shape, jnp.int32),
+            pltpu.SMEM((table.shape[0], slots, table.shape[1]), jnp.int32),
+            pltpu.VMEM((1, features), BF16),
+            pltpu.VMEM((own_rows, key_width), BF16),
+            pltpu.VMEM((replay_rows, key_width), BF16),
             pltpu.VMEM((3, half, features), BF16),
             pltpu.VMEM((3, half, features), BF16),
             pltpu.VMEM((3, half, features), BF16),
@@ -408,20 +506,24 @@
             pltpu.VMEM((replay_rows, share), BF16),
             pltpu.VMEM((replay_rows, share), BF16),
             pltpu.VMEM((ZN, XN, block, key_width), BF16),
-            pltpu.VMEM((ZN, XN - 1, block, key_width), BF16),
-            pltpu.VMEM((ZN - 1, block, key_width), BF16),
-            pltpu.VMEM((ZN - 1, block, key_width), BF16),
-            pltpu.SemaphoreType.DMA((6,)),
+            pltpu.VMEM((ZN, 2, block // 2, key_width), BF16),
+            pltpu.VMEM((ZN, 2, block // 2, key_width), BF16),
+            pltpu.VMEM((ZN, 2, block, key_width), BF16),
+            pltpu.VMEM((block, key_width), BF16),
+            pltpu.VMEM((2, block // 2, key_width), BF16),
+            pltpu.VMEM((2, block, key_width), BF16),
+            pltpu.VMEM((2, block, key_width), BF16),
+            pltpu.SemaphoreType.DMA((12,)),
             pltpu.SemaphoreType.DMA((remote,)),
             pltpu.SemaphoreType.DMA((remote,)),
         ],
         compiler_params=pltpu.CompilerParams(
-            collective_id=0, has_side_effects=True, vmem_limit_bytes=48 * 1024 * 1024
+            collective_id=0, has_side_effects=True, vmem_limit_bytes=63 * 1024 * 1024
         ),
     )(
         failed,
         counts,
-        table.reshape(table.shape[0], -1),
+        jnp.swapaxes(table, 1, 2),
         stash.reshape(2 * XN, half, features),
         own_input.reshape(own_rows, features),
         gain,

time: 123 us -> 91.8 us (0.75)
  the two profiles are of different devices: /device:TPU:12 before, /device:TPU:1 now
where the time goes in v2:
time: 91.8 us; the launch traced here: 91.4 us
  Pallas kernels  87.7 us (96%)
  local copies, waits for them, and re-layouts  3.05 us (3%)
    pallas_call x1, Pallas kernels, per_device(): pl.pallas_call(functools.partial(kernel, features * widths), out_shape=(j...  87.7 us
    unnamed x2, local copies, waits for them, and re-layouts  3.05 us

profile of v2, /device:TPU:1, one launch (start us, length us, event | category | flops | bytes accessed | tf_op | source)
XLA Modules:
  0.0 91.4 jit_solution(3918374786577565809)
XLA Ops:
  0.6 87.7 %shard_map.104 = (bf16[128,128]{1,0:T(8,128)(2,1)}, f32[128,512]{1,0:T(8,128)}) custom-call(s32[16]{0:T(128)} %failed_hbm.1, s32[16,16]{1,0:T(8,128)} %counts_hbm.1, s32[16,2,16]{2,1,0:T(2,128)} %bitcast.15, bf16[8,80,2048]{2,1,0:T(8,128)(2,1)} %bitcast.8, bf16[128,2048]{1,0:T(8,128)(2,1)} %bitcast.10, bf16[1,2048]{1,0:T(2,128)(2,1)} %gain_hbm.1, ...), custom_call_target="tpu_custom_call" | custom-call | tf_op jit(solution)/shard_map/pallas_call | solution.py:467
  88.4 1.4 %copy.13 = bf16[1,1,2,64,128]{4,3,2,1,0:T(8,128)(2,1)} copy(bf16[1,1,2,64,128]{4,3,2,1,0:T(8,128)(2,1)} %bitcast.14) | data formatting | bytes 65536
  89.7 1.7 %copy.14 = f32[1,128,512]{2,1,0:T(8,128)} copy(f32[1,128,512]{2,1,0:T(8,128)} %bitcast.11) | data formatting | bytes 524288

commit v3 on v2

--- a/solution.py
+++ b/solution.py
@@ -9,7 +9,8 @@
 MESH = pl.DeviceIdType.MESH
 XN = 4
 ZN = 4
-PIECES = 2
+PIECES = ZN
+TURNS = (2, 1, 3, 0)
 EPS = 1e-05
 F32 = jnp.float32
 BF16 = jnp.bfloat16
@@ -87,10 +88,16 @@
     cot_all,
     own_sum,
     own_sums,
+    held,
     replay_sum,
     replay_sums,
+    square_total,
+    square_x,
+    square_sent,
+    square_got,
     mixed,
     back,
+    key_total,
     key_parts,
     key_got,
     key_all,
@@ -158,10 +165,7 @@
     load_gain = load(gain_hbm, gain)
     load_own = load(own_input, own_in)
     load_cot = load(own_cotangent, own_cot)
-    load_p = load(stash.at[2 * lax.rem(x + 1, XN)], cand_p.at[0])
-    load_n = load(stash.at[2 * lax.rem(x + 3, XN) + 1], cand_n.at[0])
-    load_a = load(stash.at[2 * x], cand_a.at[0])
-    load_b = load(stash.at[2 * x + 1], cand_b.at[0])
+    load_held = load(stash, held)
     load_w = load(weight, weight_in)
 
     quarter = pl.ds(pl.multiple_of(m * share, 128), share)
@@ -191,27 +195,70 @@
         for k in range(1, XN)
     ]
 
-    far = 2 * lax.rem(x + 2, XN)
-    windows = [slice(c * features // PIECES, (c + 1) * features // PIECES) for c in range(PIECES)]
+    group = XN * block
+    windows = [
+        pl.ds(pl.multiple_of(lax.rem(z + turn, ZN) * group, 128), group) for turn in TURNS
+    ]
+    right, over, left = (lax.rem(x + k, XN) for k in range(1, XN))
     far_p, far_n, near_a, near_b = [], [], [], []
-    for w in windows:
-        far_p.append(copies.start(stash.at[far, :, w], cand_p.at[1, :, w], x_peer(1)))
-        far_n.append(copies.start(stash.at[far + 1, :, w], cand_n.at[1, :, w], x_peer(3)))
-        near = 2 * lax.rem(x + 1, XN) + 1
-        near_b.append(copies.start(stash.at[near, :, w], cand_b.at[1, :, w], x_peer(1)))
-        near = 2 * lax.rem(x + 3, XN)
-        near_a.append(copies.start(stash.at[near, :, w], cand_a.at[1, :, w], x_peer(3)))
+
+    def bulk(c):
+        w = windows[c]
+        far_p.append(copies.start(stash.at[2 * over, :, w], cand_p.at[0, :, w], x_peer(1)))
+        far_n.append(copies.start(stash.at[2 * over + 1, :, w], cand_n.at[0, :, w], x_peer(3)))
+        near_b.append(copies.start(stash.at[2 * right + 1, :, w], cand_b.at[0, :, w], x_peer(1)))
+        near_a.append(copies.start(stash.at[2 * left, :, w], cand_a.at[0, :, w], x_peer(3)))
+
+    bulk(0)
+    bulk(1)
 
     load_gain.wait()
-    scaling = gain[...].astype(F32)
     load_own.wait()
     own_float = own_in[...].astype(F32)
-    mixed[:own_rows] = (own_float * scaling).astype(BF16)
+    mixed[:own_rows] = (own_float * gain[...].astype(F32)).astype(BF16)
     column = jnp.sum(own_float * own_float, axis=1, keepdims=True)
     own_sum[...] = jnp.broadcast_to(to_row(column, own_rows), own_sum.shape)
     own_copies = [
         copies.start(own_sum, own_sums.at[k - 1], m_peer(k)) for k in range(1, widths)
     ]
+    load_held.wait()
+    padded = replay_sum.shape[1]
+    for part in range(2 * XN):
+        value = held[part].astype(F32)
+        column = jnp.sum(value * value, axis=1, keepdims=True)
+        replay_sum[part : part + 1] = to_row(column, padded)
+    sum_copies = [
+        copies.start(replay_sum, replay_sums.at[k - 1], m_peer(k)) for k in range(1, widths)
+    ]
+
+    load_failed.wait()
+    source = lax.rem(failed[upcoming], XN)
+    here = source == x
+    before = source == left
+    after = source == right
+    pass_p, pass_n, ahead = [], [], []
+
+    def relay(c):
+        w = windows[c]
+        far_p[c].wait_recv()
+        cand_p[1, :, w] = jnp.where(before, cand_p[0, :, w], held[2 * right, :, w])
+        pass_p.append(copies.start(cand_p.at[1, :, w], cand_a.at[1, :, w], x_peer(1)))
+        far_n[c].wait_recv()
+        cand_n[1, :, w] = jnp.where(after, cand_n[0, :, w], held[2 * left + 1, :, w])
+        pass_n.append(copies.start(cand_n.at[1, :, w], cand_b.at[1, :, w], x_peer(3)))
+
+    def choose(c):
+        w = windows[c]
+        near_a[c].wait_recv()
+        pass_p[c].wait_recv()
+        one = jnp.where(after, cand_a[0, :, w], cand_a[1, :, w])
+        chosen[0, :, w] = jnp.where(here, held[2 * x, :, w], one)
+        ahead.append(copies.start(chosen.at[0, :, w], arrived.at[0, :, w], {"pipe": upcoming}))
+        near_b[c].wait_recv()
+        pass_n[c].wait_recv()
+        one = jnp.where(before, cand_b[0, :, w], cand_b[1, :, w])
+        chosen[1, :, w] = jnp.where(here, held[2 * x + 1, :, w], one)
+        ahead.append(copies.start(chosen.at[1, :, w], arrived.at[1, :, w], {"pipe": upcoming}))
 
     value = cot_parts[rows_of(x)].astype(F32)
     for k, copy in enumerate(cot_copies):
@@ -220,50 +267,37 @@
     cot_sum[...] = value.astype(BF16)
     cot_copies = [copies.start(cot_sum, cot_z.at[k - 1], z_peer(k)) for k in range(1, ZN)]
 
+    total = replay_sum[...]
+    for k, copy in enumerate(sum_copies):
+        copy.wait_recv()
+        total = total + replay_sums[k]
+    square_total[...] = total
+    square_copies = [copies.start(square_total, square_x.at[k - 1], x_peer(k)) for k in range(1, XN)]
+
+    relay(0)
+    bulk(2)
+
     total = own_sum[...]
     for k, copy in enumerate(own_copies):
         copy.wait_recv()
         total = total + own_sums[k]
     factor = lax.rsqrt(total / width_total + EPS)
-    load_failed.wait()
     load_cot.wait()
     keeper = (replica != failed[section]).astype(F32)
     column = to_column(factor[:1], own_rows) * keeper
     back[:own_rows] = (own_cot[...].astype(F32) * column).astype(BF16)
 
-    source = lax.rem(failed[upcoming], XN)
-    here = source == x
-    before = source == lax.rem(x + 3, XN)
-    after = source == lax.rem(x + 1, XN)
-    load_p.wait()
-    load_n.wait()
-    pass_p, pass_n = [], []
-
-    def relay(c):
-        w = windows[c]
-        far_p[c].wait_recv()
-        cand_p[2, :, w] = jnp.where(before, cand_p[1, :, w], cand_p[0, :, w])
-        pass_p.append(copies.start(cand_p.at[2, :, w], cand_a.at[2, :, w], x_peer(1)))
-        far_n[c].wait_recv()
-        cand_n[2, :, w] = jnp.where(after, cand_n[1, :, w], cand_n[0, :, w])
-        pass_n.append(copies.start(cand_n.at[2, :, w], cand_b.at[2, :, w], x_peer(3)))
-
-    ahead = []
-
-    def choose(c):
-        w = windows[c]
-        near_a[c].wait_recv()
-        pass_p[c].wait_recv()
-        one = jnp.where(after, cand_a[1, :, w], cand_a[2, :, w])
-        chosen[0, :, w] = jnp.where(here, cand_a[0, :, w], one)
-        ahead.append(copies.start(chosen.at[0, :, w], arrived.at[0, :, w], {"pipe": upcoming}))
-        near_b[c].wait_recv()
-        pass_n[c].wait_recv()
-        one = jnp.where(before, cand_b[1, :, w], cand_b[2, :, w])
-        chosen[1, :, w] = jnp.where(here, cand_b[0, :, w], one)
-        ahead.append(copies.start(chosen.at[1, :, w], arrived.at[1, :, w], {"pipe": upcoming}))
-
-    relay(0)
+    relay(1)
+    bulk(3)
+
+    value = square_total[...]
+    for k, copy in enumerate(square_copies):
+        copy.wait_recv()
+        value = jnp.where(source == lax.rem(x + XN - 1 - k, XN), square_x[k], value)
+    square_sent[...] = value
+    square_ahead = copies.start(square_sent, square_got, {"pipe": upcoming})
+    choose(0)
+
     value = cot_sum[...].astype(F32)
     for k, copy in enumerate(cot_copies):
         copy.wait_recv()
@@ -272,83 +306,49 @@
     cot_copies = [
         copies.start(cot_all.at[m], cot_all.at[m], m_peer(k)) for k in range(1, widths)
     ]
-    load_a.wait()
-    load_b.wait()
-    for c in range(1, PIECES):
-        relay(c)
-        choose(c - 1)
+
+    relay(2)
+    choose(1)
+    relay(3)
+    choose(2)
 
     valid = (failed[section] // XN == z).astype(F32)
-    masked = scaling * valid
-    columns = [0.0, 0.0]
+    load_w.wait()
 
     def take(c):
         w = windows[c]
+        masked = gain[:, w].astype(F32) * valid
         for part in range(2):
             ahead[2 * c + part].wait_recv()
             rows = slice(own_rows + part * half, own_rows + (part + 1) * half)
-            value = arrived[part, :, w].astype(F32)
-            mixed[rows, w] = (value * masked[:, w]).astype(BF16)
-            columns[part] = columns[part] + jnp.sum(value * value, axis=1, keepdims=True)
-
-    choose(PIECES - 1)
-    load_w.wait()
-    for c in range(PIECES):
-        take(c)
-    padded = replay_sum.shape[1]
-    row = to_row(jnp.concatenate(columns, axis=0), padded)
-    replay_sum[...] = jnp.broadcast_to(row, replay_sum.shape)
-    sum_copies = [
-        copies.start(replay_sum, replay_sums.at[k - 1], m_peer(k)) for k in range(1, widths)
-    ]
-    partial = jnp.dot(mixed[own_rows:], weight_in[...], preferred_element_type=F32)
-    for place in range(widths):
-        key_parts[place] = partial[:, place * share : (place + 1) * share].astype(BF16)
-    key_copies = [
-        copies.start(key_parts.at[lax.rem(m + k, widths)], key_got.at[k - 1], m_peer(k))
-        for k in range(1, widths)
-    ]
-
-    for copy in cot_copies:
-        copy.wait_recv()
-    total = replay_sum[...]
-    for k, copy in enumerate(sum_copies):
-        copy.wait_recv()
-        total = total + replay_sums[k]
-    factor = lax.rsqrt(total / width_total + EPS)
-    column = to_column(factor[:1], chunk)
-    for place in range(widths):
-        value = cot_all[place].astype(F32) * column
-        back[own_rows:, place * share : (place + 1) * share] = value.astype(BF16)
+            mixed[rows, w] = (arrived[part, :, w].astype(F32) * masked).astype(BF16)
+        term = jnp.dot(mixed[own_rows:, w], weight_in[w], preferred_element_type=F32)
+        key_total[...] = term if c == 0 else key_total[...] + term
 
     contract = (((0,), (0,)), ((), ()))
-    group = XN * block
     middle = block // 2
     first, second = slice(0, middle), slice(middle, block)
-    turns = (2, 1, 3, 0)
     straight, passing, added = [], [], []
 
     def issue(step):
-        place = lax.rem(z + turns[step], ZN)
-        window = pl.ds(pl.multiple_of(place * group, 128), group)
+        window = windows[step]
         product = lax.dot_general(
             mixed[:, window], back[...], contract, preferred_element_type=F32
         ).astype(BF16)
         for k in range(XN):
             grad_parts[step, k] = product[k * block : (k + 1) * block]
         parts = grad_parts.at[step]
-        over = parts.at[lax.rem(x + 2, XN)]
+        distant = parts.at[over]
         passing.append(
             (
-                copies.start(over.at[first], grad_far.at[step, 0], x_peer(1)),
-                copies.start(over.at[second], grad_far.at[step, 1], x_peer(3)),
+                copies.start(distant.at[first], grad_far.at[step, 0], x_peer(1)),
+                copies.start(distant.at[second], grad_far.at[step, 1], x_peer(3)),
             )
         )
-        right, left = parts.at[lax.rem(x + 1, XN)], parts.at[lax.rem(x + 3, XN)]
         straight.append(
             (
-                copies.start(right.at[second], grad_x.at[step, 0, second], x_peer(1)),
-                copies.start(left.at[first], grad_x.at[step, 1, first], x_peer(3)),
+                copies.start(parts.at[right, second], grad_x.at[step, 0, second], x_peer(1)),
+                copies.start(parts.at[left, first], grad_x.at[step, 1, first], x_peer(3)),
             )
         )
 
@@ -370,7 +370,39 @@
         value = grad_parts[step, x].astype(F32)
         return value + grad_x[step, 0].astype(F32) + grad_x[step, 1].astype(F32)
 
+    take(0)
+    for copy in cot_copies:
+        copy.wait_recv()
+    square_ahead.wait_recv()
+    columns = []
+    for part in range(2):
+        factor = lax.rsqrt(square_got[pl.ds(2 * x + part, 1)] / width_total + EPS)
+        columns.append(to_column(factor, half))
+    column = jnp.concatenate(columns, axis=0)
+    for place in range(widths):
+        value = cot_all[place].astype(F32) * column
+        back[own_rows:, place * share : (place + 1) * share] = value.astype(BF16)
     issue(0)
+    take(1)
+    issue(1)
+    choose(3)
+    pass_on(0)
+    take(2)
+    issue(2)
+    take(3)
+
+    for place in range(widths):
+        key_parts[place] = key_total[:, place * share : (place + 1) * share].astype(BF16)
+    key_copies = [
+        copies.start(key_parts.at[lax.rem(m + k, widths)], key_got.at[k - 1], m_peer(k))
+        for k in range(1, widths)
+    ]
+    pass_on(1)
+
+    value = summed(0)
+    half_far[...] = value.astype(BF16)
+    over_p = copies.start(half_far.at[first], half_got.at[0], z_peer(1))
+    over_n = copies.start(half_far.at[second], half_got.at[1], z_peer(3))
     value = key_parts[m].astype(F32)
     for k, copy in enumerate(key_copies):
         copy.wait_recv()
@@ -380,9 +412,18 @@
         copies.start(key_all.at[rows_of(x)], key_all.at[rows_of(x)], x_peer(k))
         for k in range(1, XN)
     ]
-    issue(1)
-    pass_on(0)
-    issue(2)
+    issue(3)
+    arriving = []
+
+    value = summed(1)
+    half_send[0, second] = value[middle:].astype(BF16)
+    arriving.append(
+        copies.start(half_send.at[0, second], half_z.at[0, second], z_peer(1))
+    )
+    pass_on(2)
+    over_p.wait_recv()
+    half_send[0, first] = (value[:middle] + half_got[0].astype(F32)).astype(BF16)
+    arriving.append(copies.start(half_send.at[0, first], half_z.at[0, first], z_peer(1)))
 
     for copy in key_copies:
         copy.wait_recv()
@@ -402,24 +443,6 @@
         if k > 0:
             key_copies.append(copies.start(key_pick.at[k], key_z.at[k - 1], z_peer(k)))
 
-    value = summed(0)
-    half_far[...] = value.astype(BF16)
-    over_p = copies.start(half_far.at[first], half_got.at[0], z_peer(1))
-    over_n = copies.start(half_far.at[second], half_got.at[1], z_peer(3))
-    pass_on(1)
-    issue(3)
-    arriving = []
-
-    value = summed(1)
-    half_send[0, second] = value[middle:].astype(BF16)
-    arriving.append(
-        copies.start(half_send.at[0, second], half_z.at[0, second], z_peer(1))
-    )
-    pass_on(2)
-    over_p.wait_recv()
-    half_send[0, first] = (value[:middle] + half_got[0].astype(F32)).astype(BF16)
-    arriving.append(copies.start(half_send.at[0, first], half_z.at[0, first], z_peer(1)))
-
     value = summed(2)
     half_send[1, first] = value[:middle].astype(BF16)
     arriving.append(copies.start(half_send.at[1, first], half_z.at[1, first], z_peer(3)))
@@ -460,8 +483,8 @@
     replay_rows = slots * tokens
     block = features // (XN * ZN)
     others = max(widths - 1, 1)
-    padded = -(-chunk // 128) * 128
-    remote = 8 * PIECES + 3 + 3 + 4 * (widths - 1) + 6 * ZN + 3 + 3 + 6 + 1
+    padded = -(-half // 128) * 128
+    remote = 8 * PIECES + 4 * (widths - 1) + 6 * ZN + 3 + 3 + 3 + 1 + 3 + 3 + 1 + 6
     vmem = pl.BlockSpec(memory_space=pltpu.VMEM)
     whole = pl.BlockSpec(memory_space=pltpu.HBM)
     keys, gradient = pl.pallas_call(
@@ -479,10 +502,10 @@
             pltpu.VMEM((1, features), BF16),
             pltpu.VMEM((own_rows, key_width), BF16),
             pltpu.VMEM((replay_rows, key_width), BF16),
-            pltpu.VMEM((3, half, features), BF16),
-            pltpu.VMEM((3, half, features), BF16),
-            pltpu.VMEM((3, half, features), BF16),
-            pltpu.VMEM((3, half, features), BF16),
+            pltpu.VMEM((2, half, features), BF16),
+            pltpu.VMEM((2, half, features), BF16),
+            pltpu.VMEM((2, half, features), BF16),
+            pltpu.VMEM((2, half, features), BF16),
             pltpu.VMEM((2, half, features), BF16),
             pltpu.VMEM((2, half, features), BF16),
             pltpu.VMEM((own_rows, features), BF16),
@@ -494,10 +517,16 @@
             pltpu.VMEM((widths, chunk, share), BF16),
             pltpu.VMEM((8, own_rows), F32),
             pltpu.VMEM((others, 8, own_rows), F32),
-            pltpu.VMEM((8, padded), F32),
-            pltpu.VMEM((others, 8, padded), F32),
+            pltpu.VMEM((2 * XN, half, features), BF16),
+            pltpu.VMEM((2 * XN, padded), F32),
+            pltpu.VMEM((others, 2 * XN, padded), F32),
+            pltpu.VMEM((2 * XN, padded), F32),
+            pltpu.VMEM((XN - 1, 2 * XN, padded), F32),
+            pltpu.VMEM((2 * XN, padded), F32),
+            pltpu.VMEM((2 * XN, padded), F32),
             pltpu.VMEM((own_rows + chunk, features), BF16),
             pltpu.VMEM((own_rows + chunk, key_width), BF16),
+            pltpu.VMEM((chunk, key_width), F32),
             pltpu.VMEM((widths, chunk, share), BF16),
             pltpu.VMEM((others, chunk, share), BF16),
             pltpu.VMEM((4 * chunk, share), BF16),
@@ -513,7 +542,7 @@
             pltpu.VMEM((2, block // 2, key_width), BF16),
             pltpu.VMEM((2, block, key_width), BF16),
             pltpu.VMEM((2, block, key_width), BF16),
-            pltpu.SemaphoreType.DMA((12,)),
+            pltpu.SemaphoreType.DMA((9,)),
             pltpu.SemaphoreType.DMA((remote,)),
             pltpu.SemaphoreType.DMA((remote,)),
         ],

time: 91.8 us -> 87.7 us (0.955)
  the two profiles are of different devices: /device:TPU:1 before, /device:TPU:69 now
where the time goes in v3:
time: 87.7 us; the launch traced here: 87.5 us
  Pallas kernels  83.8 us (96%)
  local copies, waits for them, and re-layouts  3.05 us (3%)
    pallas_call x1, Pallas kernels, per_device(): pl.pallas_call(functools.partial(kernel, features * widths), out_shape=(j...  83.8 us
    unnamed x2, local copies, waits for them, and re-layouts  3.05 us

profile of v3, /device:TPU:69, one launch (start us, length us, event | category | flops | bytes accessed | tf_op | source)
XLA Modules:
  0.0 87.5 jit_solution(946932121600254420)
XLA Ops:
  0.6 83.8 %shard_map.104 = (bf16[128,128]{1,0:T(8,128)(2,1)}, f32[128,512]{1,0:T(8,128)}) custom-call(s32[16]{0:T(128)} %failed_hbm.1, s32[16,16]{1,0:T(8,128)} %counts_hbm.1, s32[16,2,16]{2,1,0:T(2,128)} %bitcast.15, bf16[8,80,2048]{2,1,0:T(8,128)(2,1)} %bitcast.8, bf16[128,2048]{1,0:T(8,128)(2,1)} %bitcast.10, bf16[1,2048]{1,0:T(2,128)(2,1)} %gain_hbm.1, ...), custom_call_target="tpu_custom_call" | custom-call | tf_op jit(solution)/shard_map/pallas_call | solution.py:490
  84.5 1.4 %copy.13 = bf16[1,1,2,64,128]{4,3,2,1,0:T(8,128)(2,1)} copy(bf16[1,1,2,64,128]{4,3,2,1,0:T(8,128)(2,1)} %bitcast.14) | data formatting | bytes 65536
  85.8 1.7 %copy.14 = f32[1,128,512]{2,1,0:T(8,128)} copy(f32[1,128,512]{2,1,0:T(8,128)} %bitcast.11) | data formatting | bytes 524288

commit v4 on v3

--- a/solution.py
+++ b/solution.py
@@ -398,6 +398,7 @@
         for k in range(1, widths)
     ]
     pass_on(1)
+    issue(3)
 
     value = summed(0)
     half_far[...] = value.astype(BF16)
@@ -412,19 +413,14 @@
         copies.start(key_all.at[rows_of(x)], key_all.at[rows_of(x)], x_peer(k))
         for k in range(1, XN)
     ]
-    issue(3)
     arriving = []
 
-    value = summed(1)
-    half_send[0, second] = value[middle:].astype(BF16)
+    pass_on(2)
+    nearer = summed(1)
+    half_send[0, second] = nearer[middle:].astype(BF16)
     arriving.append(
         copies.start(half_send.at[0, second], half_z.at[0, second], z_peer(1))
     )
-    pass_on(2)
-    over_p.wait_recv()
-    half_send[0, first] = (value[:middle] + half_got[0].astype(F32)).astype(BF16)
-    arriving.append(copies.start(half_send.at[0, first], half_z.at[0, first], z_peer(1)))
-
     for copy in key_copies:
         copy.wait_recv()
     key_copies = []
@@ -443,6 +439,11 @@
         if k > 0:
             key_copies.append(copies.start(key_pick.at[k], key_z.at[k - 1], z_peer(k)))
 
+    over_p.wait_recv()
+    half_send[0, first] = (nearer[:middle] + half_got[0].astype(F32)).astype(BF16)
+    arriving.append(copies.start(half_send.at[0, first], half_z.at[0, first], z_peer(1)))
+
+    pass_on(3)
     value = summed(2)
     half_send[1, first] = value[:middle].astype(BF16)
     arriving.append(copies.start(half_send.at[1, first], half_z.at[1, first], z_peer(3)))
@@ -452,7 +453,6 @@
         copies.start(half_send.at[1, second], half_z.at[1, second], z_peer(3))
     )
 
-    pass_on(3)
     value = key_pick[0].astype(F32)
     for k, copy in enumerate(key_copies):
         copy.wait_recv()

time: 87.7 us -> 87.4 us (level)
  the two profiles are of different devices: /device:TPU:69 before, /device:TPU:61 now
where the time goes in v4:
time: 87.4 us; the launch traced here: 87.2 us
  Pallas kernels  83.5 us (96%)
  local copies, waits for them, and re-layouts  3.05 us (3%)
    pallas_call x1, Pallas kernels, per_device(): pl.pallas_call(functools.partial(kernel, features * widths), out_shape=(j...  83.5 us
    unnamed x2, local copies, waits for them, and re-layouts  3.05 us

profile of v4, /device:TPU:61, one launch (start us, length us, event | category | flops | bytes accessed | tf_op | source)
XLA Modules:
  0.0 87.2 jit_solution(4617140799839644400)
XLA Ops:
  0.6 83.5 %shard_map.104 = (bf16[128,128]{1,0:T(8,128)(2,1)}, f32[128,512]{1,0:T(8,128)}) custom-call(s32[16]{0:T(128)} %failed_hbm.1, s32[16,16]{1,0:T(8,128)} %counts_hbm.1, s32[16,2,16]{2,1,0:T(2,128)} %bitcast.15, bf16[8,80,2048]{2,1,0:T(8,128)(2,1)} %bitcast.8, bf16[128,2048]{1,0:T(8,128)(2,1)} %bitcast.10, bf16[1,2048]{1,0:T(2,128)(2,1)} %gain_hbm.1, ...), custom_call_target="tpu_custom_call" | custom-call | tf_op jit(solution)/shard_map/pallas_call | solution.py:490
  84.1 1.4 %copy.13 = bf16[1,1,2,64,128]{4,3,2,1,0:T(8,128)(2,1)} copy(bf16[1,1,2,64,128]{4,3,2,1,0:T(8,128)(2,1)} %bitcast.14) | data formatting | bytes 65536
  85.5 1.7 %copy.14 = f32[1,128,512]{2,1,0:T(8,128)} copy(f32[1,128,512]{2,1,0:T(8,128)} %bitcast.11) | data formatting | bytes 524288
